TPU v7x, 32 devices: a whole 2x2x4 slice. The times are simulated.
32 devices in a mesh: ctx: 16 (over z, y, core), head: 2 (over x).
Axes of the slice: x: 2, y: 2, z: 4, core: 2. Of those that a mesh axis runs over, the one named last changes fastest.
Arguments:
- queries: bfloat16 [10240, 2048], P('ctx', 'head'), may hold values from -8 to 8
- keys: bfloat16 [10240, 2048], P('ctx', 'head'), may hold values from -6 to 6
- values: bfloat16 [10240, 2048], P('ctx', 'head'), may hold values from -6 to 6
- key_weight: bfloat16 [16, 16, 128], P('head'), may hold values from -1.5 to 1.5
- value_weight: bfloat16 [16, 16, 128], P('head'), may hold values from -1.5 to 1.5
Outputs:
- attended: bfloat16 [10240, 2048], P(('ctx', 'head'))
All inputs are finite; a program needn't handle non-finite values.
Results may differ from a plain program's by a relative error of at most 0.0061.
Values may be sent and summed in bfloat16 or wider, within the bound.
A program may use at most 128 MiB of HBM per device.

v0:
```python
import functools
import math

import jax
import jax.numpy as jnp
import numpy as np
from jax import lax
from jax.experimental import pallas as pl
from jax.experimental.pallas import tpu as pltpu
from jax.sharding import PartitionSpec as P

WINDOW = 3


def kernel(dims, q_hbm, k_hbm, v_hbm, kw_ref, vw_ref, bias_ref, out_hbm,
           q_own, kv_own, far, comp, acc, top, stage,
           own_sem, send_sem, recv_sem, comp_send, comp_recv, out_send, out_recv, out_local):
    n_ctx, n_head, heads, rows, width, group, padded = dims
    bits = n_ctx.bit_length() - 1
    groups = rows // group
    part_rows = rows // n_head
    half = rows // 2
    scale = math.log2(math.e) / math.sqrt(width)
    me, side = lax.axis_index("ctx"), lax.axis_index("head")

    def partner(bit):
        step = 1 << bit
        return me + (1 - 2 * ((me // step) % 2)) * step

    def columns(h):
        return pl.ds(pl.multiple_of(h * width, width), width)

    def own_copy(i, h):
        src = (k_hbm, v_hbm, q_hbm)[i].at[:, columns(h)]
        dst = q_own.at[h] if i == 2 else kv_own.at[i, h]
        return pltpu.make_async_copy(src, dst, own_sem.at[i, h])

    def kv_copy(bit, i, h):
        return pltpu.make_async_remote_copy(
            src_ref=(k_hbm, v_hbm)[i].at[:, columns(h)],
            dst_ref=far.at[bit, i, h],
            send_sem=send_sem.at[bit, i, h],
            recv_sem=recv_sem.at[bit, i, h],
            device_id={"ctx": partner(bit)},
            device_id_type=pl.DeviceIdType.MESH,
        )

    def comp_copy(step):
        count = 1 << step
        return pltpu.make_async_remote_copy(
            src_ref=comp.at[pl.ds(0, count)],
            dst_ref=comp.at[pl.ds(count, count)],
            send_sem=comp_send.at[step],
            recv_sem=comp_recv.at[step],
            device_id={"ctx": partner(bits - 1 - step)},
            device_id_type=pl.DeviceIdType.MESH,
        )

    def out_columns(h):
        return pl.ds(pl.multiple_of((side * heads + h) * width, width), width)

    def out_copy(d, h):
        peer = (side + d) % n_head
        return pltpu.make_async_remote_copy(
            src_ref=stage.at[h, pl.ds(pl.multiple_of(peer * part_rows, part_rows), part_rows)],
            dst_ref=out_hbm.at[:, out_columns(h)],
            send_sem=out_send.at[d - 1, h],
            recv_sem=out_recv.at[d - 1, h],
            device_id={"head": peer},
            device_id_type=pl.DeviceIdType.MESH,
        )

    def out_own(h):
        return pltpu.make_async_copy(
            stage.at[h, pl.ds(pl.multiple_of(side * part_rows, part_rows), part_rows)],
            out_hbm.at[:, out_columns(h)],
            out_local.at[h],
        )

    def send_head(h):
        for bit in reversed(range(bits)):
            for i in range(2):
                kv_copy(bit, i, h).start()

    barrier = pltpu.get_barrier_semaphore()
    for bit in range(bits):
        pl.semaphore_signal(barrier, inc=1, device_id={"ctx": partner(bit)},
                            device_id_type=pl.DeviceIdType.MESH)
    for d in range(1, n_head):
        pl.semaphore_signal(barrier, inc=1, device_id={"head": (side + d) % n_head},
                            device_id_type=pl.DeviceIdType.MESH)

    @pl.loop(0, heads)
    def _(h):
        for i in range(3):
            own_copy(i, h).start()

    pl.semaphore_wait(barrier, bits + n_head - 1)
    send_head(0)

    @pl.loop(0, heads)
    def _(h):
        for i, weight in enumerate((kw_ref, vw_ref)):
            own_copy(i, h).wait()
            grouped = kv_own[i, h].astype(jnp.float32).reshape(groups, group, width)
            folded = jnp.sum(grouped * weight[h].astype(jnp.float32)[None], axis=1)
            if padded > groups:
                folded = jnp.concatenate(
                    [folded, jnp.zeros((padded - groups, width), jnp.float32)], 0)
            comp[0, i, h] = folded.astype(jnp.bfloat16)
        own_copy(2, h).wait()

    def attend(h, key_rows, value_rows, bias=None, first=False, last=False):
        ones = jnp.ones((value_rows.shape[0], width), jnp.bfloat16)
        wide = jnp.concatenate([value_rows, ones], 1)
        for t in range(2):
            span = pl.ds(t * half, half)
            scores = lax.dot_general(q_own[h, span], key_rows, (((1,), (1,)), ((), ())),
                                     preferred_element_type=jnp.float32) * scale
            if bias is not None:
                scores = scores + bias
            new_top = jnp.max(scores, axis=1, keepdims=True)
            if not first:
                old_top = top[h, span]
                new_top = jnp.maximum(new_top, old_top)
            weights = jnp.exp2(scores - new_top).astype(jnp.bfloat16)
            summed = jnp.dot(weights, wide, preferred_element_type=jnp.float32)
            if not first:
                summed = summed + acc[h, span] * jnp.exp2(old_top - new_top)
            if last:
                stage[h, span] = (summed[:, :width] / summed[:, width:]).astype(jnp.bfloat16)
            else:
                acc[h, span] = summed
                top[h, span] = new_top

    cuts = [heads * s // bits for s in range(bits + 1)]
    for step in range(bits):
        comp_copy(step).start()
        if step + 1 < min(WINDOW, heads):
            send_head(step + 1)

        @pl.loop(cuts[step], cuts[step + 1])
        def _(h):
            attend(h, kv_own[0, h], kv_own[1, h], first=True)

        comp_copy(step).wait_recv()

    order = list(range(bits))

    @pl.loop(0, heads)
    def _(h):
        flat = n_ctx * padded
        attend(h, comp[:, 0, h].reshape(flat, width), comp[:, 1, h].reshape(flat, width),
               bias=bias_ref[0:1, :])
        for bit in order:
            for i in range(2):
                kv_copy(bit, i, h).wait_recv()
            if bit == order[-1]:
                @pl.when(h + WINDOW < heads)
                def _():
                    send_head(h + WINDOW)
            attend(h, far[bit, 0, h], far[bit, 1, h], last=bit == order[-1])
        for d in range(1, n_head):
            out_copy(d, h).start()
        out_own(h).start()

    for step in range(bits):
        comp_copy(step).wait_send()

    @pl.loop(0, heads)
    def _(h):
        for bit in range(bits):
            for i in range(2):
                kv_copy(bit, i, h).wait_send()
        for d in range(1, n_head):
            out_copy(d, h).wait()
        out_own(h).wait()


def body(n_ctx, n_head, queries, keys, values, key_weight, value_weight):
    rows, channels = queries.shape
    heads, group, width = key_weight.shape
    bits = n_ctx.bit_length() - 1
    groups = rows // group
    padded = -(-groups // 16) * 16
    dims = (n_ctx, n_head, heads, rows, width, group, padded)
    flat = n_ctx * padded
    bias = np.where(np.arange(flat) % padded < groups, 0.0, -np.inf).astype(np.float32)
    bias = jnp.asarray(np.broadcast_to(bias, (8, flat)))
    dma = pltpu.SemaphoreType.DMA
    anywhere = pl.BlockSpec(memory_space=pl.ANY)
    vmem = pl.BlockSpec(memory_space=pltpu.VMEM)
    pairs = rows * heads * (bits + 1) * rows + rows * heads * flat
    return pl.pallas_call(
        functools.partial(kernel, dims),
        out_shape=jax.ShapeDtypeStruct((rows // n_head, channels * n_head), jnp.bfloat16),
        in_specs=[anywhere] * 3 + [vmem] * 3,
        out_specs=anywhere,
        scratch_shapes=[
            pltpu.VMEM((heads, rows, width), jnp.bfloat16),
            pltpu.VMEM((2, heads, rows, width), jnp.bfloat16),
            pltpu.VMEM((bits, 2, heads, rows, width), jnp.bfloat16),
            pltpu.VMEM((n_ctx, 2, heads, padded, width), jnp.bfloat16),
            pltpu.VMEM((heads, rows, 2 * width), jnp.float32),
            pltpu.VMEM((heads, rows, 1), jnp.float32),
            pltpu.VMEM((heads, rows, width), jnp.bfloat16),
            dma((3, heads)),
            dma((bits, 2, heads)),
            dma((bits, 2, heads)),
            dma((bits,)),
            dma((bits,)),
            dma((n_head - 1, heads)),
            dma((n_head - 1, heads)),
            dma((heads,)),
        ],
        compiler_params=pltpu.CompilerParams(
            collective_id=0, has_side_effects=True, vmem_limit_bytes=56 * 1024 * 1024),
        cost_estimate=pl.CostEstimate(
            flops=4 * pairs * width, bytes_accessed=8 * rows * channels, transcendentals=pairs),
    )(queries, keys, values, key_weight, value_weight, bias)


def solution(mesh):
    in_specs = (
        P("ctx", "head"),
        P("ctx", "head"),
        P("ctx", "head"),
        P("head", None, None),
        P("head", None, None),
    )
    out_specs = P(("ctx", "head"), None)
    inner = functools.partial(body, mesh.shape["ctx"], mesh.shape["head"])
    return jax.shard_map(inner, mesh=mesh, in_specs=in_specs, out_specs=out_specs, check_vma=False)
```

profile of v0, /device:TPU:9, one launch (start us, length us, event | category | flops | bytes accessed | tf_op | source)
XLA Modules:
  0.0 160.5 jit_solution(15162058962226110101)
XLA Ops:
  0.0 1.3 jit_solution_.3.bias_ref
  1.3 156.7 %shard_map.64 = bf16[320,2048]{1,0:T(8,128)(2,1)} custom-call(bf16[640,1024]{1,0:T(8,128)(2,1)} %q_hbm.1, bf16[640,1024]{1,0:T(8,128)(2,1)} %k_hbm.1, bf16[640,1024]{1,0:T(8,128)(2,1)} %v_hbm.1, bf16[8,16,128]{2,1,0:T(8,128)(2,1)} %kw_ref.1, bf16[8,16,128]{2,1,0:T(8,128)(2,1)} %vw_ref.1, f32[8,768]{1,0:T(8,128)} %jit_solution_.3.bias_ref), custom_call_target="tpu_custom_call" | custom-call | flops 10401873920 | bytes 5242880 | tf_op jit(solution)/shard_map/pallas_call | solution.py:194
  158.0 2.5 %copy.8 = bf16[320,2048]{1,0:T(8,128)(2,1)} copy(bf16[320,2048]{1,0:T(8,128)(2,1)} %shard_map.64) | data formatting | bytes 2621440
where the time goes:
time: 161 us; the launch traced here: 160 us
  Pallas kernels  157 us (98%)
  local copies, waits for them, and re-layouts  3.82 us (2%)
    pallas_call x1, Pallas kernels, body(): pl.pallas_call(functools.partial(kernel, dims), out_shape=jax.ShapeDtypeS...  157 us

commit v1 on v0

--- a/solution.py
+++ b/solution.py
@@ -3,16 +3,16 @@
 
 import jax
 import jax.numpy as jnp
-import numpy as np
 from jax import lax
 from jax.experimental import pallas as pl
 from jax.experimental.pallas import tpu as pltpu
 from jax.sharding import PartitionSpec as P
 
-WINDOW = 3
-
-
-def kernel(dims, q_hbm, k_hbm, v_hbm, kw_ref, vw_ref, bias_ref, out_hbm,
+FAR_WINDOW = 5
+NEAR_WINDOW = 5
+
+
+def kernel(dims, q_hbm, k_hbm, v_hbm, kw_ref, vw_ref, out_hbm,
            q_own, kv_own, far, comp, acc, top, stage,
            own_sem, send_sem, recv_sem, comp_send, comp_recv, out_send, out_recv, out_local):
     n_ctx, n_head, heads, rows, width, group, padded = dims
@@ -77,10 +77,20 @@
             out_local.at[h],
         )
 
-    def send_head(h):
+    windows = [min(heads, NEAR_WINDOW)] * (bits - 1) + [min(heads, FAR_WINDOW)]
+
+    def send_first(h):
         for bit in reversed(range(bits)):
-            for i in range(2):
-                kv_copy(bit, i, h).start()
+            if h < windows[bit]:
+                for i in range(2):
+                    kv_copy(bit, i, h).start()
+
+    def send_next(h):
+        for bit in reversed(range(bits)):
+            @pl.when(h + windows[bit] < heads)
+            def _():
+                for i in range(2):
+                    kv_copy(bit, i, h + windows[bit]).start()
 
     barrier = pltpu.get_barrier_semaphore()
     for bit in range(bits):
@@ -96,7 +106,7 @@
             own_copy(i, h).start()
 
     pl.semaphore_wait(barrier, bits + n_head - 1)
-    send_head(0)
+    send_first(0)
 
     @pl.loop(0, heads)
     def _(h):
@@ -136,8 +146,8 @@
     cuts = [heads * s // bits for s in range(bits + 1)]
     for step in range(bits):
         comp_copy(step).start()
-        if step + 1 < min(WINDOW, heads):
-            send_head(step + 1)
+        for h in range(step + 1, step + 2 if step + 1 < bits else heads):
+            send_first(h)
 
         @pl.loop(cuts[step], cuts[step + 1])
         def _(h):
@@ -150,15 +160,15 @@
     @pl.loop(0, heads)
     def _(h):
         flat = n_ctx * padded
+        place = lax.broadcasted_iota(jnp.int32, (1, flat), 1)
+        bias = jnp.where(lax.rem(place, padded) < groups, 0.0, -jnp.inf)
         attend(h, comp[:, 0, h].reshape(flat, width), comp[:, 1, h].reshape(flat, width),
-               bias=bias_ref[0:1, :])
+               bias=bias)
         for bit in order:
             for i in range(2):
                 kv_copy(bit, i, h).wait_recv()
             if bit == order[-1]:
-                @pl.when(h + WINDOW < heads)
-                def _():
-                    send_head(h + WINDOW)
+                send_next(h)
             attend(h, far[bit, 0, h], far[bit, 1, h], last=bit == order[-1])
         for d in range(1, n_head):
             out_copy(d, h).start()
@@ -185,8 +195,6 @@
     padded = -(-groups // 16) * 16
     dims = (n_ctx, n_head, heads, rows, width, group, padded)
     flat = n_ctx * padded
-    bias = np.where(np.arange(flat) % padded < groups, 0.0, -np.inf).astype(np.float32)
-    bias = jnp.asarray(np.broadcast_to(bias, (8, flat)))
     dma = pltpu.SemaphoreType.DMA
     anywhere = pl.BlockSpec(memory_space=pl.ANY)
     vmem = pl.BlockSpec(memory_space=pltpu.VMEM)
@@ -194,7 +202,7 @@
     return pl.pallas_call(
         functools.partial(kernel, dims),
         out_shape=jax.ShapeDtypeStruct((rows // n_head, channels * n_head), jnp.bfloat16),
-        in_specs=[anywhere] * 3 + [vmem] * 3,
+        in_specs=[anywhere] * 3 + [vmem] * 2,
         out_specs=anywhere,
         scratch_shapes=[
             pltpu.VMEM((heads, rows, width), jnp.bfloat16),
@@ -217,7 +225,7 @@
             collective_id=0, has_side_effects=True, vmem_limit_bytes=56 * 1024 * 1024),
         cost_estimate=pl.CostEstimate(
             flops=4 * pairs * width, bytes_accessed=8 * rows * channels, transcendentals=pairs),
-    )(queries, keys, values, key_weight, value_weight, bias)
+    )(queries, keys, values, key_weight, value_weight)
 
 
 def solution(mesh):

time: 161 us -> 142 us (0.88)
  the two profiles are of different devices: /device:TPU:9 before, /device:TPU:0 now
where the time goes in v1:
time: 142 us
  Pallas kernels  140 us (99%)
  local copies, waits for them, and re-layouts  2.52 us (2%)
    pallas_call x1, Pallas kernels, body(): pl.pallas_call(functools.partial(kernel, dims), out_shape=jax.ShapeDtypeS...  140 us

profile of v1, /device:TPU:0, one launch (start us, length us, event | category | flops | bytes accessed | tf_op | source)
XLA Modules:
  0.0 142.2 jit_solution(5384827734451518849)
XLA Ops:
  0.0 139.7 %shard_map.55 = bf16[320,2048]{1,0:T(8,128)(2,1)} custom-call(bf16[640,1024]{1,0:T(8,128)(2,1)} %q_hbm.1, bf16[640,1024]{1,0:T(8,128)(2,1)} %k_hbm.1, bf16[640,1024]{1,0:T(8,128)(2,1)} %v_hbm.1, bf16[8,16,128]{2,1,0:T(8,128)(2,1)} %kw_ref.1, bf16[8,16,128]{2,1,0:T(8,128)(2,1)} %vw_ref.1), custom_call_target="tpu_custom_call" | custom-call | flops 10401873920 | bytes 5242880 | tf_op jit(solution)/shard_map/pallas_call | solution.py:202
  139.7 2.5 %copy.7 = bf16[320,2048]{1,0:T(8,128)(2,1)} copy(bf16[320,2048]{1,0:T(8,128)(2,1)} %shard_map.55) | data formatting | bytes 2621440

commit v2 on v1

--- a/solution.py
+++ b/solution.py
@@ -8,7 +8,8 @@
 from jax.experimental.pallas import tpu as pltpu
 from jax.sharding import PartitionSpec as P
 
-FAR_WINDOW = 5
+FAR_WINDOW = 6
+SKEW = 2
 NEAR_WINDOW = 5
 
 
@@ -85,8 +86,8 @@
                 for i in range(2):
                     kv_copy(bit, i, h).start()
 
-    def send_next(h):
-        for bit in reversed(range(bits)):
+    def send_next(h, chosen):
+        for bit in reversed(chosen):
             @pl.when(h + windows[bit] < heads)
             def _():
                 for i in range(2):
@@ -155,24 +156,35 @@
 
         comp_copy(step).wait_recv()
 
-    order = list(range(bits))
-
-    @pl.loop(0, heads)
-    def _(h):
-        flat = n_ctx * padded
-        place = lax.broadcasted_iota(jnp.int32, (1, flat), 1)
-        bias = jnp.where(lax.rem(place, padded) < groups, 0.0, -jnp.inf)
-        attend(h, comp[:, 0, h].reshape(flat, width), comp[:, 1, h].reshape(flat, width),
-               bias=bias)
-        for bit in order:
+    def take(h, chosen):
+        for bit in chosen:
             for i in range(2):
                 kv_copy(bit, i, h).wait_recv()
-            if bit == order[-1]:
-                send_next(h)
-            attend(h, far[bit, 0, h], far[bit, 1, h], last=bit == order[-1])
-        for d in range(1, n_head):
-            out_copy(d, h).start()
-        out_own(h).start()
+            if bit == chosen[-1]:
+                send_next(h, chosen)
+            attend(h, far[bit, 0, h], far[bit, 1, h], last=bit == bits - 1)
+
+    skew = min(heads, SKEW)
+
+    @pl.loop(0, heads + skew)
+    def _(turn):
+        @pl.when(turn < heads)
+        def _():
+            h = turn
+            flat = n_ctx * padded
+            place = lax.broadcasted_iota(jnp.int32, (1, flat), 1)
+            bias = jnp.where(lax.rem(place, padded) < groups, 0.0, -jnp.inf)
+            attend(h, comp[:, 0, h].reshape(flat, width), comp[:, 1, h].reshape(flat, width),
+                   bias=bias)
+            take(h, list(range(bits - 2)))
+
+        @pl.when(turn >= skew)
+        def _():
+            h = turn - skew
+            take(h, [bits - 2, bits - 1])
+            for d in range(1, n_head):
+                out_copy(d, h).start()
+            out_own(h).start()
 
     for step in range(bits):
         comp_copy(step).wait_send()

time: 142 us -> 142 us (level)
  no operation moved by 1% of the time
where the time goes in v2:
time: 142 us
  Pallas kernels  140 us (99%)
  local copies, waits for them, and re-layouts  2.52 us (2%)
    pallas_call x1, Pallas kernels, body(): pl.pallas_call(functools.partial(kernel, dims), out_shape=jax.ShapeDtypeS...  140 us

profile of v2, /device:TPU:0, one launch (start us, length us, event | category | flops | bytes accessed | tf_op | source)
XLA Modules:
  0.0 142.3 jit_solution(1677968134576245684)
XLA Ops:
  0.0 139.8 %shard_map.55 = bf16[320,2048]{1,0:T(8,128)(2,1)} custom-call(bf16[640,1024]{1,0:T(8,128)(2,1)} %q_hbm.1, bf16[640,1024]{1,0:T(8,128)(2,1)} %k_hbm.1, bf16[640,1024]{1,0:T(8,128)(2,1)} %v_hbm.1, bf16[8,16,128]{2,1,0:T(8,128)(2,1)} %kw_ref.1, bf16[8,16,128]{2,1,0:T(8,128)(2,1)} %vw_ref.1), custom_call_target="tpu_custom_call" | custom-call | flops 10401873920 | bytes 5242880 | tf_op jit(solution)/shard_map/pallas_call | solution.py:214
  139.8 2.5 %copy.7 = bf16[320,2048]{1,0:T(8,128)(2,1)} copy(bf16[320,2048]{1,0:T(8,128)(2,1)} %shard_map.55) | data formatting | bytes 2621440
